TPU v7x, 32 devices: a whole 2x2x4 slice. The times are simulated.
32 devices in a mesh: groups: 2 (over y), dp: 4 (over z), tensor: 4 (over x, core).
Axes of the slice: x: 2, y: 2, z: 4, core: 2. Of those that a mesh axis runs over, the one named last changes fastest.
Arguments:
- tokens: bfloat16 [6144, 8192], P(('groups', 'dp'), 'tensor'), parts along dimension 0, may hold values from -6 to 6
- value_weight_frozen: bfloat16 [8192, 1024], P('tensor'), may hold values from -0.0625 to 0.0625
- adapter_down_weight: bfloat16 [8192, 128], P('tensor', ('groups', 'dp')), parts along dimension 1, may hold values from -0.0625 to 0.0625
- adapter_up_weight: bfloat16 [1024, 128], P('tensor', ('groups', 'dp')), parts along dimension 1, may hold values from -1.5 to 1.5
- slot_adapter_index: int32 [6144], P(('groups', 'dp')), parts along dimension 0, may hold values from 0 to 3, never falling along the last dimension, each value on 1 to 1536 neighbouring positions
- adapter_owner_slot: int32 [8], P('groups'), parts along dimension 0, may hold values from 0 to 3, each once
- balanced_row_index: int32 [6144], P(('groups', 'dp')), parts along dimension 0, may hold values from -1 to 1535, as said below
- cotangent: bfloat16 [3072, 1024], P(('groups', 'dp'), 'tensor'), parts along dimension 0, may hold values from -0.119628906 to 0.119628906
Outputs:
- projected: bfloat16 [3072, 1024], P(('groups', 'dp'), 'tensor'), parts along dimension 0
- grad_down: float32 [8192, 128], P('tensor', ('groups', 'dp')), parts along dimension 1
- grad_up: float32 [1024, 128], P('tensor', ('groups', 'dp')), parts along dimension 1
There are 2 independent parts, one for each index of `groups`. A program takes and returns all parts, laid end to end along the dimension named above; an argument that names none is the same for every part. Nothing has to cross between parts.
Inputs may be any that keep to these rules, and one draw needn't show every extreme that they name: `balanced_row_index`: each index of dp holds its live slots first and -1 after them; every balanced row 0 to 1535 is named by exactly one slot; the live slots of one index of dp name at most 192 rows of any one block of 384 balanced rows, and some index names exactly 192 rows of some block in every draw; some index of dp has all 768 slots live. `slot_adapter_index`: never falls along the token slots; each adapter holds 1 to 1536 slots, one exactly 1536. `adapter_owner_slot`: each owner slot exactly once.
All inputs are finite; a program needn't handle non-finite values.
Results may differ from a plain program's by a relative error of at most 0.0055.
Values may be sent and summed in bfloat16 or wider, within the bound.
A program may use at most 64 MiB of HBM per device.

v0:
```python
import jax
import jax.numpy as jnp
from jax import lax
from jax.sharding import PartitionSpec as P

SCALE = 2.0


def spread(onehot, values):
    row_count = values.shape[0]
    return (onehot[:, :, None] * values[:, None, :]).reshape(
        row_count, onehot.shape[1] * values.shape[1]
    )


def select_rank(dense, onehot):
    row_count, count_cols = onehot.shape
    return jnp.sum(dense.reshape(row_count, count_cols, -1) * onehot[:, :, None], axis=1)


def body(
    tokens,
    value_weight_frozen,
    adapter_down_weight,
    adapter_up_weight,
    slot_adapter_index,
    adapter_owner_slot,
    balanced_row_index,
    cotangent,
):
    peer_count = lax.axis_size("dp")
    slot_count, shard_width = tokens.shape
    balanced, value_width = cotangent.shape
    capacity = slot_count // peer_count
    adapters = adapter_owner_slot.shape[0]
    adapter_range = jnp.arange(adapters, dtype=jnp.int32)
    owner_slot = jnp.sum(
        jnp.where(
            slot_adapter_index[:, None] == adapter_range[None, :], adapter_owner_slot[None, :], 0
        ),
        axis=1,
    )
    is_live = balanced_row_index >= 0
    target = jnp.where(is_live, balanced_row_index // balanced, peer_count)
    dest_hits = (target[:, None] == jnp.arange(peer_count, dtype=jnp.int32)[None, :]).astype(
        jnp.int32
    )
    within = jnp.sum(jnp.cumsum(dest_hits, axis=0) * dest_hits, axis=1) - 1
    bucket_pos = jnp.where(is_live, target * capacity + within, peer_count * capacity)
    send_rows = (
        jnp.zeros((peer_count * capacity, shard_width), tokens.dtype)
        .at[bucket_pos]
        .set(tokens, mode="drop")
    )
    send_local = (
        jnp.full((peer_count * capacity,), balanced, jnp.int32)
        .at[bucket_pos]
        .set(balanced_row_index % balanced, mode="drop")
    )
    send_owner = (
        jnp.zeros((peer_count * capacity,), jnp.int32).at[bucket_pos].set(owner_slot, mode="drop")
    )
    got_rows, got_local, got_owner = (
        lax.all_to_all(
            send_rows.reshape(peer_count, capacity, shard_width),
            "dp",
            split_axis=0,
            concat_axis=0,
            tiled=True,
        ),
        lax.all_to_all(
            send_local.reshape(peer_count, capacity), "dp", split_axis=0, concat_axis=0, tiled=True
        ),
        lax.all_to_all(
            send_owner.reshape(peer_count, capacity), "dp", split_axis=0, concat_axis=0, tiled=True
        ),
    )
    got_local = got_local.reshape(-1)
    rows_bal = (
        jnp.zeros((balanced, shard_width), tokens.dtype)
        .at[got_local]
        .set(got_rows.reshape(-1, shard_width), mode="drop")
    )
    owner_bal = (
        jnp.zeros((balanced,), jnp.int32).at[got_local].set(got_owner.reshape(-1), mode="drop")
    )
    down_gathered, up_gathered = (
        lax.all_gather(adapter_down_weight, "dp", axis=1, tiled=True),
        lax.all_gather(adapter_up_weight, "dp", axis=1, tiled=True),
    )
    onehot = (owner_bal[:, None] == adapter_range[None, :]).astype(jnp.float32)
    down_projected = jnp.dot(rows_bal, down_gathered, preferred_element_type=jnp.float32)
    low_part = select_rank(down_projected, onehot)
    base_part = jnp.dot(rows_bal, value_weight_frozen, preferred_element_type=jnp.float32)
    cotangent_proj = jnp.dot(cotangent, up_gathered, preferred_element_type=jnp.float32)
    grad_part = select_rank(cotangent_proj, onehot)
    low_full = lax.psum(low_part, "tensor")
    summed = lax.psum_scatter(base_part, "tensor", scatter_dimension=1, tiled=True)
    lifted = jnp.einsum(
        "ba,ka->bk",
        spread(onehot, low_full),
        up_gathered.astype(jnp.float32),
        precision=lax.Precision.HIGHEST,
    )
    projected = (summed + SCALE * lifted).astype(jnp.bfloat16)
    grad_full = lax.psum(grad_part, "tensor")
    low_half = low_full.astype(jnp.bfloat16)
    grad_half = grad_full.astype(jnp.bfloat16)
    mask_half = onehot.astype(jnp.bfloat16)
    grad_spread = spread(mask_half, grad_half)
    low_spread = spread(mask_half, low_half)
    down_term = SCALE * jnp.einsum(
        "bd,ba->da", rows_bal, grad_spread, preferred_element_type=jnp.float32
    )
    up_term = SCALE * jnp.einsum(
        "bk,ba->ka", cotangent, low_spread, preferred_element_type=jnp.float32
    )
    grad_down, grad_up = (
        lax.psum_scatter(down_term, "dp", scatter_dimension=1, tiled=True),
        lax.psum_scatter(up_term, "dp", scatter_dimension=1, tiled=True),
    )
    return (projected, grad_down, grad_up)


def solution(mesh):
    return jax.shard_map(
        body,
        mesh=mesh,
        in_specs=(
            P(("groups", "dp"), "tensor"),
            P("tensor", None),
            P("tensor", ("groups", "dp")),
            P("tensor", ("groups", "dp")),
            P(("groups", "dp")),
            P("groups"),
            P(("groups", "dp")),
            P(("groups", "dp"), "tensor"),
        ),
        out_specs=(
            P(("groups", "dp"), "tensor"),
            P("tensor", ("groups", "dp")),
            P("tensor", ("groups", "dp")),
        ),
        check_vma=False,
    )
```

profile of v0, /device:TPU:1, one launch (start us, length us, event | category | flops | bytes accessed | tf_op | source)
XLA Modules:
  0.0 219.3 jit_solution(6693590744774175884)
XLA Ops:
  7.2 0.7 add_select_fusion
  7.9 1.1 reduce-window.6
  9.1 0.2 slice_reduce_fusion
  9.3 0.2 reduce-window.9
  9.5 0.1 add_bitcast_fusion
  9.6 0.7 compare_select_fusion.1
  10.3 3.4 %scatter_custom_fusion = s32[768]{0:T(1024)S(1)} fusion(s32[768]{0:T(1024)S(1)} %compare_select_fusion.1, s32[768]{0:T(1024)S(1)} %get-tuple-element.7, s32[]{:T(128)} %constant.15.clone.1), kind=kCustom, calls=%fused_computation.44 | custom fusion | bytes 3076 | tf_op jit(solution)/shard_map/scatter | solution.py:58
  13.7 0.7 all_to_all.15
  14.3 5.4 %all-to-all-start = ((s32[4,1,192]{2,1,0:T(1,128)}), s32[4,1,192]{2,1,0:T(1,128)S(1)}, u32[]{:S(2)}, u32[]{:S(2)}) async-start(s32[4,1,192]{2,1,0:T(1,128)} %all_to_all.15), calls=%async_computation | async-start | bytes 8192 | tf_op jit(solution)/shard_map/all_to_all | solution.py:71
  19.8 9.9 %scatter_custom_fusion.1 = bf16[768,2048]{1,0:T(8,128)(2,1)} fusion(s32[768]{0:T(1024)S(1)} %compare_select_fusion.1, bf16[768,2048]{1,0:T(8,128)(2,1)} %param.8, bf16[]{:T(256)} %constant.14.clone.1), kind=kCustom, calls=%fused_computation.6 | custom fusion | bytes 3146240 | tf_op jit(solution)/shard_map/scatter | solution.py:53
  29.7 4.5 %all-to-all-start.1 = ((bf16[4,192,2048]{2,1,0:T(8,128)(2,1)}), bf16[4,192,2048]{2,1,0:T(8,128)(2,1)S(1)}, u32[]{:S(2)}, u32[]{:S(2)}) async-start(bf16[4,192,2048]{2,1,0:T(8,128)(2,1)} %bitcast.2), calls=%async_computation.1 | async-start | bytes 6291456 | tf_op jit(solution)/shard_map/all_to_all | solution.py:64
  34.2 0.1 reshape.136
  34.3 70.0 %all-to-all-done.1 = bf16[4,192,2048]{2,1,0:T(8,128)(2,1)S(1)} async-done(((bf16[4,192,2048]{2,1,0:T(8,128)(2,1)}), bf16[4,192,2048]{2,1,0:T(8,128)(2,1)S(1)}, u32[]{:S(2)}, u32[]{:S(2)}) %all-to-all-start.1) | async-done | bytes 3145760 | tf_op jit(solution)/shard_map/all_to_all | solution.py:64
  104.4 1.7 copy-done.1
  106.0 8.4 %scatter_custom_fusion.2 = bf16[384,2048]{1,0:T(8,128)(2,1)S(1)} fusion(s32[768]{0:T(1024)S(1)} %fusion.13, bf16[768,2048]{1,0:T(8,128)(2,1)} %bitcast.38, bf16[]{:T(256)} %constant.14.clone.1), kind=kCustom, calls=%fused_computation.13 | custom fusion | bytes 1573376 | tf_op jit(solution)/shard_map/scatter | solution.py:82
  114.5 5.2 %fusion.22 = f32[384,1024]{1,0:T(8,128)} fusion(bf16[384,2048]{1,0:T(8,128)(2,1)S(1)} %scatter_custom_fusion.2, bf16[2048,1024]{1,0:T(8,128)(2,1)} %param.9), kind=kOutput, calls=%fused_computation.50 | convolution fusion | flops 1610612736 | bytes 7340032 | tf_op jit(solution)/shard_map/dot_general | solution.py:94
  119.7 0.1 select_reduce_fusion
  119.8 3.4 %scatter_custom_fusion.3 = s32[768]{0:T(1024)S(1)} fusion(s32[768]{0:T(1024)S(1)} %compare_select_fusion.1, s32[768]{0:T(1024)S(1)} %select_reduce_fusion, s32[]{:T(128)} %constant.16.clone.1), kind=kCustom, calls=%fused_computation.41 | custom fusion | bytes 3076 | tf_op jit(solution)/shard_map/scatter | solution.py:61
  123.1 0.7 all_to_all.18
  123.8 3.2 %all-to-all-start.2 = ((s32[4,1,192]{2,1,0:T(1,128)}), s32[4,1,192]{2,1,0:T(1,128)S(1)}, u32[]{:S(2)}, u32[]{:S(2)}) async-start(s32[4,1,192]{2,1,0:T(1,128)} %all_to_all.18), calls=%async_computation.3 | async-start | bytes 8192 | tf_op jit(solution)/shard_map/all_to_all | solution.py:74
  127.1 10.4 %all_gather.7 = bf16[256,64]{0,1:T(8,128)(2,1)S(1)} all-gather(bf16[256,16]{0,1:T(8,128)(2,1)S(1)} %copy-done.3), channel_id=1, replica_groups=mesh['groups'=2,'dp'=4,'tensor'=4] {'dp'}, dimensions={1}, use_global_device_ids=true | all-gather | bytes 40960 | tf_op jit(solution)/shard_map/all_gather | solution.py:89
  137.5 0.2 fusion.24
  137.7 11.3 %all_gather.6 = bf16[2048,64]{0,1:T(8,128)(2,1)S(1)} all-gather(bf16[2048,16]{0,1:T(8,128)(2,1)S(1)} %copy-done.2), channel_id=1, replica_groups=mesh['groups'=2,'dp'=4,'tensor'=4] {'dp'}, dimensions={1}, use_global_device_ids=true | all-gather | bytes 327680 | tf_op jit(solution)/shard_map/all_gather | solution.py:88
  149.0 0.1 reshape.178
  149.1 3.4 %scatter_custom_fusion.4 = s32[384]{0:T(512)S(1)} fusion(s32[768]{0:T(1024)S(1)} %fusion.13, s32[768]{0:T(1024)S(1)} %reshape.178, s32[]{:T(128)} %constant.16.clone.1), kind=kCustom, calls=%fused_computation.46 | custom fusion | bytes 1540 | tf_op jit(solution)/shard_map/scatter | solution.py:85
  152.5 0.6 fusion.23
  153.1 17.6 %all-reduce = (f32[384,16]{0,1:T(8,128)S(1)}, bf16[384,16]{0,1:T(8,128)(2,1)S(1)}) all-reduce(f32[384,16]{0,1:T(8,128)S(1)} %get-tuple-element.4, f32[384,16]{0,1:T(8,128)S(1)} %get-tuple-element.3), channel_id=1, replica_groups=mesh['groups'=2,'dp'=4,'tensor'=4] {'tensor'}, use_global_device_ids=true, to_apply=%region_11.12 | all-reduce | flops 12288 | bytes 86016 | tf_op jit(solution)/shard_map/psum | solution.py:97
  170.7 0.8 fusion.4
  171.6 1.2 convolution_multiply_fusion
  172.9 2.0 fusion.3
  174.9 14.6 %reduce-scatter.8.cloned.1.call-done = f32[256,16]{0,1:T(8,128)} async-done(((f32[256,64]{0,1:T(8,128)}), f32[256,16]{0,1:T(8,128)}) %reduce-scatter.8.cloned.1.call-update) | async-done | bytes 16400 | tf_op jit(solution)/shard_map/reduce_scatter | solution.py:120
  189.6 23.3 %reduce-scatter.6.cloned.1.call-done = f32[2048,16]{0,1:T(8,128)} async-done(((f32[2048,64]{0,1:T(8,128)}), f32[2048,16]{0,1:T(8,128)}) %reduce-scatter.6.cloned.1.call-update) | async-done | bytes 131088 | tf_op jit(solution)/shard_map/reduce_scatter | solution.py:119
  (30 shorter events, 0.3 us)
Async XLA Ops:
  7.2 130.4 %copy-start = (bf16[384,256]{1,0:T(8,128)(2,1)S(1)}, bf16[384,256]{1,0:T(8,128)(2,1)}, u32[]{:S(2)}) copy-start(bf16[384,256]{1,0:T(8,128)(2,1)} %param.15) | copy-start | bytes 589828
  14.3 15.3 %all-to-all-start = ((s32[4,1,192]{2,1,0:T(1,128)}), s32[4,1,192]{2,1,0:T(1,128)S(1)}, u32[]{:S(2)}, u32[]{:S(2)}) async-start(s32[4,1,192]{2,1,0:T(1,128)} %all_to_all.15), calls=%async_computation | async-start | bytes 8192 | tf_op jit(solution)/shard_map/all_to_all | solution.py:71
  29.7 74.7 %all-to-all-start.1 = ((bf16[4,192,2048]{2,1,0:T(8,128)(2,1)}), bf16[4,192,2048]{2,1,0:T(8,128)(2,1)S(1)}, u32[]{:S(2)}, u32[]{:S(2)}) async-start(bf16[4,192,2048]{2,1,0:T(8,128)(2,1)} %bitcast.2), calls=%async_computation.1 | async-start | bytes 6291456 | tf_op jit(solution)/shard_map/all_to_all | solution.py:64
  34.2 138.7 %reduce-scatter.4.cloned.1.call-start = ((), (), s32[]{:S(2)}) async-start(), calls=%async_computation.6 | async-start | bytes 1966080 | tf_op jit(solution)/shard_map/reduce_scatter | solution.py:98
  104.4 1.7 copy-start.1
  114.4 5.2 %copy-start.4 = (s32[768]{0:T(1024)S(1)}, s32[768]{0:T(1024)}, u32[]{:S(2)}) copy-start(s32[768]{0:T(1024)} %param.12) | copy-start | bytes 9220
  114.4 5.2 %copy-start.5 = (s32[4]{0:T(128)S(1)}, s32[4]{0:T(128)}, u32[]{:S(2)}) copy-start(s32[4]{0:T(128)} %param.13) | copy-start | bytes 52
  114.4 12.7 %copy-start.3 = (bf16[256,16]{0,1:T(8,128)(2,1)S(1)}, bf16[256,16]{0,1:T(8,128)(2,1)}, u32[]{:S(2)}) copy-start(bf16[256,16]{0,1:T(8,128)(2,1)} %param.11) | copy-start | bytes 24580
  114.5 23.3 %copy-start.2 = (bf16[2048,16]{0,1:T(8,128)(2,1)S(1)}, bf16[2048,16]{0,1:T(8,128)(2,1)}, u32[]{:S(2)}) copy-start(bf16[2048,16]{0,1:T(8,128)(2,1)} %param.10) | copy-start | bytes 196612
  123.8 25.2 %all-to-all-start.2 = ((s32[4,1,192]{2,1,0:T(1,128)}), s32[4,1,192]{2,1,0:T(1,128)S(1)}, u32[]{:S(2)}, u32[]{:S(2)}) async-start(s32[4,1,192]{2,1,0:T(1,128)} %all_to_all.18), calls=%async_computation.3 | async-start | bytes 8192 | tf_op jit(solution)/shard_map/all_to_all | solution.py:74
  127.1 62.5 %reduce-scatter.8.cloned.1.call-start = ((), (), s32[]{:S(2)}) async-start(), calls=%async_computation.8 | async-start | bytes 81920 | tf_op jit(solution)/shard_map/reduce_scatter | solution.py:120
  171.6 41.3 %reduce-scatter.6.cloned.1.call-start = ((), (), s32[]{:S(2)}) async-start(), calls=%async_computation.7 | async-start | bytes 655360 | tf_op jit(solution)/shard_map/reduce_scatter | solution.py:119
Sparse Core Ops, SparseCore 0:
  119.8 28.0 reduce-scatter.3
  171.7 17.8 reduce-scatter.7
  192.4 20.3 reduce-scatter.5
where the time goes:
time: 222 us; the launch traced here: 219 us
  waiting for transfers between devices  108 us (49%)
  blocking collectives  39.2 us (18%)
  local copies, waits for them, and re-layouts  31.8 us (14%)
  between operations  13.9 us (6%)
  starting transfers between devices  13.3 us (6%)
  matrix products  9.99 us (4%)
  other arithmetic  3.08 us (1%)
    all_to_all x1, waiting for transfers between devices, body(): lax.all_to_all(send_rows.reshape(peer_count, capacity, shard_width), 'dp'...  70 us
    reduce_scatter x1, waiting for transfers between devices, body(): lax.psum_scatter(down_term, 'dp', scatter_dimension=1, tiled=True)  23.3 us
    psum x1, blocking collectives, body(): low_full = lax.psum(low_part, 'tensor')  17.6 us
    reduce_scatter x1, waiting for transfers between devices, body(): lax.psum_scatter(up_term, 'dp', scatter_dimension=1, tiled=True)  14.6 us
    all_gather x1, blocking collectives, body(): lax.all_gather(adapter_down_weight, 'dp', axis=1, tiled=True)  11.3 us
    all_gather x1, blocking collectives, body(): lax.all_gather(adapter_up_weight, 'dp', axis=1, tiled=True)  10.4 us
    scatter x1, local copies, waits for them, and re-layouts, body(): send_rows = jnp.zeros((peer_count * capacity, shard_width), tokens.dtype)...  9.89 us
    scatter x1, local copies, waits for them, and re-layouts, body(): rows_bal = jnp.zeros((balanced, shard_width), tokens.dtype).at[got_local]...  8.39 us
  transfers between devices with their start and end apart: 6, of which 3 were waited for; matrix products, arithmetic and copies ran while one was open for 10% of the time, Pallas kernels for 0%

commit v1 on v0

v1 whole, which is shorter than its diff:
```python
import functools

import jax
import jax.numpy as jnp
from jax import lax
from jax.experimental import pallas as pl
from jax.experimental.pallas import tpu as pltpu
from jax.sharding import PartitionSpec as P

SCALE = 2.0
RANK = 16
F32 = jnp.float32
BF16 = jnp.bfloat16
MESH = pl.DeviceIdType.MESH

NN = (((1,), (0,)), ((), ()))
NT = (((1,), (1,)), ((), ()))
TN = (((0,), (0,)), ((), ()))


def mm(a, b, dims=NN):
    return lax.dot_general(a, b, dims, preferred_element_type=F32)


def onehot(cond):
    return jnp.where(cond, 1.0, 0.0).astype(BF16)


def kernel(
    n, T, G, adapters,
    slot_ref, tok_hbm, w_hbm, fac_ref, sidx_ref, bidx_ref, cot_ref,
    out_ref, grad_ref,
    tok, w, rows, fac_all, cot_all, cotb,
    sib_send, sib_recv, own, x_send, x_recv,
    low_send, low_recv, gl_send, gl_recv,
    z_send, z_recv, zm_send, zm_recv, g_send, g_recv,
    local_sem, fac_ss, fac_rs, cot_ss, cot_rs, sib_ss, sib_rs, x_ss, x_rs,
    low_ss, low_rs, gl_ss, gl_rs, z_ss, z_rs, zm_ss, zm_rs, g_ss, g_rs,
):
    me = lax.axis_index("dp")
    q = lax.axis_index("tensor")
    slots, depth = tok.shape
    bal, vw = out_ref.shape
    cap = z_send.shape[1]
    H = T // 2
    per = n // G
    chunk = per * cap
    half = q // 2
    parity = lax.rem(q, 2)

    def peer_dp(k):
        return lax.rem(me + k, n)

    def peer_t(k):
        return lax.rem(q + k, T)

    loads = [pltpu.make_async_copy(tok_hbm, tok, local_sem.at[T])]
    for k in range(H):
        for own_side in range(2):
            par = parity if own_side else 1 - parity
            block = 2 * lax.rem(half + k, H) + par
            loads.append(
                pltpu.make_async_copy(
                    w_hbm.at[:, pl.ds(pl.multiple_of(block * vw, vw), vw)],
                    w.at[own_side * H + k],
                    local_sem.at[own_side * H + k],
                )
            )
    for c in loads:
        c.start()

    barrier = pltpu.get_barrier_semaphore()
    for k in range(1, n):
        pl.semaphore_signal(barrier, inc=1, device_id={"dp": peer_dp(k)}, device_id_type=MESH)
    for k in range(1, T):
        pl.semaphore_signal(barrier, inc=1, device_id={"tensor": peer_t(k)}, device_id_type=MESH)
    fac_all[me] = fac_ref[...]
    cot_all[me] = cot_ref[...]
    pl.semaphore_wait(barrier, n - 1 + T - 1)

    def line(buf, ss, rs):
        def send(k):
            for way in range(2):
                if way == 0:
                    block, to = me - k + 1, me + 1
                    ok = jnp.logical_and(block >= 0, to < n)
                else:
                    block, to = me + k - 1, me - 1
                    ok = jnp.logical_and(block < n, to >= 0)
                at = jnp.clip(block, 0, n - 1)
                tgt = jnp.clip(to, 0, n - 1)

                @pl.when(ok)
                def _():
                    pltpu.make_async_remote_copy(
                        src_ref=buf.at[at], dst_ref=buf.at[at],
                        send_sem=ss.at[way, k - 1], recv_sem=rs.at[way, k - 1],
                        device_id={"dp": tgt}, device_id_type=MESH,
                    ).start()

        def finish(k, sending):
            for way in range(2):
                if sending:
                    block = me - k + 1 if way == 0 else me + k - 1
                    to = me + 1 if way == 0 else me - 1
                    ok = jnp.logical_and(
                        jnp.logical_and(block >= 0, block < n),
                        jnp.logical_and(to >= 0, to < n),
                    )
                else:
                    block = me - k if way == 0 else me + k
                    ok = jnp.logical_and(block >= 0, block < n)
                at = jnp.clip(block, 0, n - 1)
                tgt = jnp.where(me > 0, me - 1, me + 1)

                @pl.when(ok)
                def _():
                    c = pltpu.make_async_remote_copy(
                        src_ref=buf.at[at], dst_ref=buf.at[at],
                        send_sem=ss.at[way, k - 1], recv_sem=rs.at[way, k - 1],
                        device_id={"dp": tgt}, device_id_type=MESH,
                    )
                    if sending:
                        c.wait_send()
                    else:
                        c.wait_recv()

        def advance(k):
            finish(k, False)
            if k < n - 1:
                send(k + 1)

        return send, finish, advance

    fac_step, fac_finish, fac_advance = line(fac_all, fac_ss, fac_rs)
    cot_step, cot_finish, cot_advance = line(cot_all, cot_ss, cot_rs)
    fac_step(1)
    cot_step(1)

    npad = max(16, n)
    bidx = bidx_ref[...]
    kio = lax.broadcasted_iota(jnp.int32, (npad, slots), 0)
    dest = lax.rem(me + 1 + kio, n)
    first = jnp.where(kio < n, dest * bal, 1 << 24)
    hit = jnp.logical_and(bidx >= first, bidx < first + bal)
    tri = onehot(
        lax.broadcasted_iota(jnp.int32, (slots, slots), 0)
        < lax.broadcasted_iota(jnp.int32, (slots, slots), 1)
    )
    rank = mm(onehot(hit), tri)
    place = jnp.where(hit, rank, -1.0)
    loc1 = jnp.sum(jnp.where(hit, bidx - first + 1, 0), axis=0, keepdims=True)
    sidx = sidx_ref[...]
    owner1 = jnp.zeros((1, slots), jnp.int32)
    for a in range(adapters):
        owner1 = jnp.where(sidx == a, slot_ref[a] + 1, owner1)
    rio = lax.broadcasted_iota(jnp.int32, (16, slots), 0)
    meta = jnp.where(
        rio == 0, loc1 >> 4, jnp.where(rio == 1, loc1 & 15, jnp.where(rio == 2, owner1, 0))
    ).astype(F32).astype(BF16)

    iota_cap = lax.broadcasted_iota(jnp.int32, (cap, slots), 0).astype(F32)
    loc_cols, own_rows = [], []

    def sib_copy(g):
        return pltpu.make_async_remote_copy(
            src_ref=sib_send.at[g], dst_ref=sib_recv.at[g],
            send_sem=sib_ss.at[g], recv_sem=sib_rs.at[g],
            device_id={"tensor": q + 1 - 2 * parity}, device_id_type=MESH,
        )

    def x_copy(g, k):
        return pltpu.make_async_remote_copy(
            src_ref=x_send.at[g, k - 1], dst_ref=x_recv.at[g, k - 1],
            send_sem=x_ss.at[g, k - 1], recv_sem=x_rs.at[g, k - 1],
            device_id={"tensor": 2 * lax.rem(half + k, H) + parity}, device_id_type=MESH,
        )

    def sum_pair(g):
        sib_copy(g).wait_recv()
        for k in list(range(1, H)) + [0]:
            total = own[g, k] + sib_recv[g, k].astype(F32)
            if k == 0:
                own[g, 0] = total
            else:
                x_send[g, k - 1] = total.astype(BF16)
                x_copy(g, k).start()

    steps = [k for k in range(1, n)]
    for g in range(G):
        parts = []
        for k in range(g * per, (g + 1) * per):
            b = onehot(iota_cap == place[k:k + 1, :])
            parts.append(b)
            row = mm(meta, b, NT)
            zm_send[k] = jnp.broadcast_to(row[0:1] * 16.0 + row[1:2], (8, cap))
            col = mm(b, meta, NT)
            loc_cols.append(col[:, 0:1] * 16.0 + col[:, 1:2])
        bg = parts[0] if per == 1 else jnp.concatenate(parts, axis=0)
        own_rows.append(mm(meta, bg, NT)[2:3] - 1.0)
        if g == 0:
            loads[0].wait()
        rows[g] = mm(bg, tok[...]).astype(BF16)
        for k in range(H):
            if g == 0:
                loads[1 + 2 * k].wait()
            sib_send[g, k] = mm(rows[g], w[k]).astype(BF16)
        sib_copy(g).start()
        for k in range(H):
            if g == 0:
                loads[2 + 2 * k].wait()
            own[g, k] = mm(rows[g], w[H + k])
        if g > 0:
            sum_pair(g - 1)
        for k in steps[g * (n - 1) // G:(g + 1) * (n - 1) // G]:
            fac_advance(k)
            cot_advance(k)

    def select(dense, g):
        total = jnp.zeros((RANK, chunk), F32)
        for p in range(n):
            total = total + jnp.where(
                own_rows[g] == float(p), dense[p * RANK:(p + 1) * RANK, :], 0.0
            )
        return total

    def spread(values, g):
        return jnp.concatenate(
            [jnp.where(own_rows[g] == float(p), values, 0.0) for p in range(n)], axis=0
        )

    def low_copy(k, send, recv, ss, rs):
        return pltpu.make_async_remote_copy(
            src_ref=send, dst_ref=recv.at[k - 1],
            send_sem=ss.at[k - 1], recv_sem=rs.at[k - 1],
            device_id={"tensor": peer_t(k)}, device_id_type=MESH,
        )

    down = fac_all[:, :, :depth].reshape(n * RANK, depth)
    up = fac_all[:, :, depth:].reshape(n * RANK, vw)
    for g in range(G):
        low_send[g] = select(mm(down, rows[g], NT), g)
    for k in range(1, T):
        low_copy(k, low_send, low_recv, low_ss, low_rs).start()
    sum_pair(G - 1)

    for g in range(G):
        for i in range(per):
            k = g * per + i
            col = loc_cols[k]
            pick = onehot(
                col == (lax.broadcasted_iota(jnp.int32, (cap, bal), 1) + 1).astype(F32)
            )
            cotb[g, i * cap:(i + 1) * cap, :] = mm(pick, cot_all[peer_dp(k + 1)]).astype(BF16)
        gl_send[g] = select(mm(up, cotb[g], NT), g)
    for k in range(1, T):
        low_copy(k, gl_send, gl_recv, gl_ss, gl_rs).start()

    def z_copy(k, send, recv, ss, rs):
        return pltpu.make_async_remote_copy(
            src_ref=send.at[k], dst_ref=recv.at[k],
            send_sem=ss.at[k], recv_sem=rs.at[k],
            device_id={"dp": peer_dp(k + 1)}, device_id_type=MESH,
        )

    for k in range(n - 1):
        z_copy(k, zm_send, zm_recv, zm_ss, zm_rs).start()

    for k in range(1, T):
        low_copy(k, low_send, low_recv, low_ss, low_rs).wait_recv()
    up_twice = jnp.concatenate([up, up], axis=0)
    low_spreads = []
    for g in range(G):
        low = low_send[g]
        for k in range(T - 1):
            low = low + low_recv[k, g]
        high = low.astype(BF16)
        rest = low - high.astype(F32)
        high_s = spread(high.astype(F32), g).astype(BF16)
        low_spreads.append(high_s)
        both = jnp.concatenate([high_s, spread(rest, g).astype(BF16)], axis=0)
        total = own[g, 0] + SCALE * mm(both, up_twice, TN)
        for k in range(1, H):
            x_copy(g, k).wait_recv()
            total = total + x_recv[g, k - 1].astype(F32)
        done = total.astype(BF16)
        for i in range(per):
            k = g * per + i
            z_send[k] = done[i * cap:(i + 1) * cap, :]
            if k < n - 1:
                z_copy(k, z_send, z_recv, z_ss, z_rs).start()

    for k in range(1, T):
        low_copy(k, gl_send, gl_recv, gl_ss, gl_rs).wait_recv()
    d_down = jnp.zeros((n * RANK, depth), F32)
    d_up = jnp.zeros((n * RANK, vw), F32)
    for g in range(G):
        gl = gl_send[g]
        for k in range(T - 1):
            gl = gl + gl_recv[k, g]
        gl_s = spread(gl.astype(BF16).astype(F32), g).astype(BF16)
        d_down = d_down + mm(gl_s, rows[g])
        d_up = d_up + mm(low_spreads[g], cotb[g])
    g_send[:, :, :depth] = (SCALE * d_down).astype(BF16).reshape(n, RANK, depth)
    g_send[:, :, depth:] = (SCALE * d_up).astype(BF16).reshape(n, RANK, vw)

    def g_copy(k):
        return pltpu.make_async_remote_copy(
            src_ref=g_send.at[peer_dp(k)], dst_ref=g_recv.at[k - 1],
            send_sem=g_ss.at[k - 1], recv_sem=g_rs.at[k - 1],
            device_id={"dp": peer_dp(k)}, device_id_type=MESH,
        )

    for k in range(1, n):
        g_copy(k).start()

    jio = (lax.broadcasted_iota(jnp.int32, (bal, cap), 0) + 1).astype(F32)
    result = mm(onehot(zm_send[n - 1][0:1] == jio), z_send[n - 1])
    for k in range(n - 1):
        z_copy(k, zm_send, zm_recv, zm_ss, zm_rs).wait_recv()
        z_copy(k, z_send, z_recv, z_ss, z_rs).wait_recv()
        result = result + mm(onehot(zm_recv[k][0:1] == jio), z_recv[k])
    out_ref[...] = result.astype(BF16)

    total = g_send[me].astype(F32)
    for k in range(1, n):
        g_copy(k).wait_recv()
        total = total + g_recv[k - 1].astype(F32)
    grad_ref[...] = total

    for k in range(1, n):
        fac_finish(k, True)
        cot_finish(k, True)
        g_copy(k).wait_send()
        z_copy(k - 1, zm_send, zm_recv, zm_ss, zm_rs).wait_send()
        z_copy(k - 1, z_send, z_recv, z_ss, z_rs).wait_send()
    for g in range(G):
        sib_copy(g).wait_send()
        for k in range(1, H):
            x_copy(g, k).wait_send()
    for k in range(1, T):
        low_copy(k, low_send, low_recv, low_ss, low_rs).wait_send()
        low_copy(k, gl_send, gl_recv, gl_ss, gl_rs).wait_send()


def body(n, T, tokens, weight, down, up, slot_adapter, owner_slot, balanced, cotangent):
    slots, depth = tokens.shape
    bal, vw = cotangent.shape
    adapters = owner_slot.shape[0]
    cap = -(-(slots // n) // 16) * 16
    G = 4 if n % 4 == 0 else n
    chunk = n // G * cap
    H = T // 2
    factors = jnp.concatenate([down.T, up.T], axis=1)
    vmem, hbm = pl.BlockSpec(memory_space=pltpu.VMEM), pl.BlockSpec(memory_space=pl.ANY)
    dma = pltpu.SemaphoreType.DMA
    projected, grads = pl.pallas_call(
        functools.partial(kernel, n, T, G, adapters),
        out_shape=(
            jax.ShapeDtypeStruct((bal, vw), BF16),
            jax.ShapeDtypeStruct((RANK, depth + vw), F32),
        ),
        in_specs=[pl.BlockSpec(memory_space=pltpu.SMEM), hbm, hbm, vmem, vmem, vmem, vmem],
        out_specs=(vmem, vmem),
        scratch_shapes=[
            pltpu.VMEM((slots, depth), BF16),
            pltpu.VMEM((T, depth, vw), BF16),
            pltpu.VMEM((G, chunk, depth), BF16),
            pltpu.VMEM((n, RANK, depth + vw), BF16),
            pltpu.VMEM((n, bal, vw), BF16),
            pltpu.VMEM((G, chunk, vw), BF16),
            pltpu.VMEM((G, H, chunk, vw), BF16),
            pltpu.VMEM((G, H, chunk, vw), BF16),
            pltpu.VMEM((G, H, chunk, vw), F32),
            pltpu.VMEM((G, H - 1, chunk, vw), BF16),
            pltpu.VMEM((G, H - 1, chunk, vw), BF16),
            pltpu.VMEM((G, RANK, chunk), F32),
            pltpu.VMEM((T - 1, G, RANK, chunk), F32),
            pltpu.VMEM((G, RANK, chunk), F32),
            pltpu.VMEM((T - 1, G, RANK, chunk), F32),
            pltpu.VMEM((n, cap, vw), BF16),
            pltpu.VMEM((n, cap, vw), BF16),
            pltpu.VMEM((n, 8, cap), F32),
            pltpu.VMEM((n, 8, cap), F32),
            pltpu.VMEM((n, RANK, depth + vw), BF16),
            pltpu.VMEM((n, RANK, depth + vw), BF16),
            dma((T + 1,)),
            dma((2, n - 1)), dma((2, n - 1)), dma((2, n - 1)), dma((2, n - 1)),
            dma((G,)), dma((G,)), dma((G, H - 1)), dma((G, H - 1)),
            dma((T - 1,)), dma((T - 1,)), dma((T - 1,)), dma((T - 1,)),
            dma((n - 1,)), dma((n - 1,)), dma((n - 1,)), dma((n - 1,)),
            dma((n - 1,)), dma((n - 1,)),
        ],
        compiler_params=pltpu.CompilerParams(
            collective_id=0, has_side_effects=True, vmem_limit_bytes=48 * 1024 * 1024
        ),
        name="value_lora",
    )(
        owner_slot, tokens, weight, factors,
        slot_adapter.reshape(1, slots), balanced.reshape(1, slots), cotangent,
    )
    return projected, grads[:, :depth].T, grads[:, depth:].T


def solution(mesh):
    rows = ("groups", "dp")
    return jax.shard_map(
        functools.partial(body, mesh.shape["dp"], mesh.shape["tensor"]),
        mesh=mesh,
        in_specs=(
            P(rows, "tensor"), P("tensor", None), P("tensor", rows), P("tensor", rows),
            P(rows), P("groups"), P(rows), P(rows, "tensor"),
        ),
        out_specs=(P(rows, "tensor"), P("tensor", rows), P("tensor", rows)),
        check_vma=False,
    )
```

time: 222 us -> 52.7 us (0.24); the launches traced: 219 us -> 52.4 us
  waiting for transfers between devices: 108 us -> 0 us
  Pallas kernels: 0 us -> 44.1 us
  blocking collectives: 39.2 us -> 0 us
  local copies, waits for them, and re-layouts: 31.8 us -> 6.8 us
  starting transfers between devices: 13.3 us -> 0 us
  between operations: 13.9 us -> 0.64 us
  matrix products: 9.99 us -> 0 us
  other arithmetic: 3.08 us -> 0.86 us
    all_to_all x3 -> x0, waiting for transfers between devices: 70 us -> none  [the longest x1 70 us: body(): lax.all_to_all(send_rows.reshape(peer_count, capacity, shard_width), 'dp'...]
    pallas_call x0 -> x1, Pallas kernels: none -> 44.1 us  [body(): pl.pallas_call(functools.partial(kernel, n, T, G, adapters), out_shape=(j...]
    reduce_scatter x3 -> x0, waiting for transfers between devices: 37.9 us -> none  [the longest x1 23.3 us: body(): lax.psum_scatter(down_term, 'dp', scatter_dimension=1, tiled=True)]
    scatter x5 -> x0, local copies, waits for them, and re-layouts: 28.4 us -> none  [the longest x1 9.89 us: body(): send_rows = jnp.zeros((peer_count * capacity, shard_width), tokens.dtype)...]
    all_gather x2 -> x0, blocking collectives: 21.7 us -> none  [the longest x1 11.3 us: body(): lax.all_gather(adapter_down_weight, 'dp', axis=1, tiled=True)]
    psum x1 -> x0, blocking collectives: 17.6 us -> none  [body(): low_full = lax.psum(low_part, 'tensor')]
    all_to_all x3 -> x0, starting transfers between devices: 13.2 us -> none  [the longest x1 5.42 us: body(): lax.all_to_all(send_local.reshape(peer_count, capacity), 'dp', split_axis...]
    dot_general x6 -> x0, matrix products: 9.99 us -> none  [the longest x1 5.16 us: body(): jnp.dot(rows_bal, value_weight_frozen, preferred_element_type=jnp.float32)]
  transfers between devices with their start and end apart: 6 -> 0, of which waited for: 3 -> 0; matrix products, arithmetic and copies ran while one was open for 10% -> 0% of each run, Pallas kernels for 0% -> 0%
where the time goes in v1:
time: 52.7 us; the launch traced here: 52.4 us
  Pallas kernels  44.1 us (84%)
  local copies, waits for them, and re-layouts  6.8 us (13%)
  other arithmetic  0.86 us (2%)
  between operations  0.64 us (1%)
    pallas_call x1, Pallas kernels, body(): pl.pallas_call(functools.partial(kernel, n, T, G, adapters), out_shape=(j...  44.1 us
    unnamed x7, local copies, waits for them, and re-layouts  4.15 us
    transpose x2, local copies, waits for them, and re-layouts, body(): return (projected, grads[:, :depth].T, grads[:, depth:].T)  1.27 us

profile of v1, /device:TPU:1, one launch (start us, length us, event | category | flops | bytes accessed | tf_op | source)
XLA Modules:
  0.0 52.4 jit_solution(8953732598068031204)
XLA Ops:
  0.6 0.7 %reshape.12.sidx_ref = s32[1,768]{1,0:T(1,128)S(1)} reshape(s32[768]{0:T(1024)} %param.12) | data formatting | bytes 6144 | tf_op jit(solution)/shard_map/reshape | solution.py:400
  1.3 0.7 %reshape.13.bidx_ref = s32[1,768]{1,0:T(1,128)S(1)} reshape(s32[768]{0:T(1024)} %param.14) | data formatting | bytes 6144 | tf_op jit(solution)/shard_map/reshape | solution.py:400
  2.0 0.9 %pad_maximum_fusion.fac_ref = bf16[16,2304]{1,0:T(8,128)(2,1)S(1)} fusion(bf16[16,256]{1,0:T(8,128)(2,1)} %bitcast.7, bf16[16,2048]{1,0:T(8,128)(2,1)} %bitcast.6), kind=kLoop, calls=%fused_computation.1 | loop fusion | flops 147456 | bytes 147456 | tf_op jit(solution)/shard_map/concatenate | solution.py:354
  2.9 0.0 copy-start
  2.9 1.9 %copy-done = bf16[768,2048]{1,0:T(8,128)(2,1)S(1)} copy-done((bf16[768,2048]{1,0:T(8,128)(2,1)S(1)}, bf16[768,2048]{1,0:T(8,128)(2,1)}, u32[]{:S(2)}) %copy-start) | copy-done | bytes 3145752
  4.8 0.0 copy-start.1
  4.8 0.9 %copy-done.1 = bf16[384,256]{1,0:T(8,128)(2,1)S(1)} copy-done((bf16[384,256]{1,0:T(8,128)(2,1)S(1)}, bf16[384,256]{1,0:T(8,128)(2,1)}, u32[]{:S(2)}) %copy-start.1) | copy-done | bytes 196632
  5.7 0.0 copy-start.2
  5.7 0.7 %copy-done.2 = s32[4]{0:T(128)S(1)} copy-done((s32[4]{0:T(128)S(1)}, s32[4]{0:T(128)}, u32[]{:S(2)}) %copy-start.2) | copy-done | bytes 40
  6.3 44.1 %value_lora.1 = (bf16[384,256]{1,0:T(8,128)(2,1)S(1)}, f32[16,2304]{1,0:T(8,128)S(1)}) custom-call(s32[4]{0:T(128)S(1)} %copy-done.2, bf16[768,2048]{1,0:T(8,128)(2,1)S(1)} %copy-done, bf16[2048,1024]{1,0:T(8,128)(2,1)} %w_hbm.1, bf16[16,2304]{1,0:T(8,128)(2,1)S(1)} %pad_maximum_fusion.fac_ref, s32[1,768]{1,0:T(1,128)S(1)} %reshape.12.sidx_ref, ...), custom_call_target="tpu_custom_call" | custom-call | tf_op jit(solution)/shard_map/value_lora/pallas_call | solution.py:357
  50.5 0.6 %slice_bitcast_fusion.1 = f32[256,16]{0,1:T(8,128)} fusion(f32[16,2304]{1,0:T(8,128)S(1)} %get-tuple-element.6), kind=kLoop, calls=%fused_computation.2 | loop fusion | bytes 32768 | tf_op jit(solution)/shard_map/transpose | solution.py:402
  51.1 0.7 %slice_bitcast_fusion = f32[2048,16]{0,1:T(8,128)} fusion(f32[16,2304]{1,0:T(8,128)S(1)} %get-tuple-element.6), kind=kLoop, calls=%fused_computation | loop fusion | bytes 262144 | tf_op jit(solution)/shard_map/transpose | solution.py:402
  51.8 0.7 %copy.12 = bf16[384,256]{1,0:T(8,128)(2,1)} copy(bf16[384,256]{1,0:T(8,128)(2,1)S(1)} %get-tuple-element.10) | data formatting | bytes 393216
Async XLA Ops:
  2.9 1.9 %copy-start = (bf16[768,2048]{1,0:T(8,128)(2,1)S(1)}, bf16[768,2048]{1,0:T(8,128)(2,1)}, u32[]{:S(2)}) copy-start(bf16[768,2048]{1,0:T(8,128)(2,1)} %tok_hbm.1) | copy-start | bytes 9437188
  4.8 0.9 %copy-start.1 = (bf16[384,256]{1,0:T(8,128)(2,1)S(1)}, bf16[384,256]{1,0:T(8,128)(2,1)}, u32[]{:S(2)}) copy-start(bf16[384,256]{1,0:T(8,128)(2,1)} %cot_ref.1) | copy-start | bytes 589828
  5.7 0.7 %copy-start.2 = (s32[4]{0:T(128)S(1)}, s32[4]{0:T(128)}, u32[]{:S(2)}) copy-start(s32[4]{0:T(128)} %slot_ref.1) | copy-start | bytes 52

commit v2 on v1

--- a/solution.py
+++ b/solution.py
@@ -28,13 +28,13 @@
 
 def kernel(
     n, T, G, adapters,
-    slot_ref, tok_hbm, w_hbm, fac_ref, sidx_ref, bidx_ref, cot_ref,
-    out_ref, grad_ref,
-    tok, w, rows, fac_all, cot_all, cotb,
+    slot_hbm, tok_hbm, w_hbm, down_hbm, up_hbm, sidx_hbm, bidx_hbm, cot_hbm,
+    out_ref, down_out, up_out,
+    slot_ref, sidx_ref, bidx_ref, tok, w, rows, fac_all, cot_all, cotb,
     sib_send, sib_recv, own, x_send, x_recv,
     low_send, low_recv, gl_send, gl_recv,
     z_send, z_recv, zm_send, zm_recv, g_send, g_recv,
-    local_sem, fac_ss, fac_rs, cot_ss, cot_rs, sib_ss, sib_rs, x_ss, x_rs,
+    small_sem, local_sem, fac_ss, fac_rs, cot_ss, cot_rs, sib_ss, sib_rs, x_ss, x_rs,
     low_ss, low_rs, gl_ss, gl_rs, z_ss, z_rs, zm_ss, zm_rs, g_ss, g_rs,
 ):
     me = lax.axis_index("dp")
@@ -54,6 +54,19 @@
     def peer_t(k):
         return lax.rem(q + k, T)
 
+    small = [
+        pltpu.make_async_copy(src, dst, small_sem.at[i])
+        for i, (src, dst) in enumerate((
+            (down_hbm, fac_all.at[me, :, pl.ds(0, depth)]),
+            (up_hbm, fac_all.at[me, :, pl.ds(depth, vw)]),
+            (slot_hbm, slot_ref),
+            (sidx_hbm, sidx_ref),
+            (bidx_hbm, bidx_ref),
+            (cot_hbm, cot_all.at[me]),
+        ))
+    ]
+    for c in small:
+        c.start()
     loads = [pltpu.make_async_copy(tok_hbm, tok, local_sem.at[T])]
     for k in range(H):
         for own_side in range(2):
@@ -74,8 +87,6 @@
         pl.semaphore_signal(barrier, inc=1, device_id={"dp": peer_dp(k)}, device_id_type=MESH)
     for k in range(1, T):
         pl.semaphore_signal(barrier, inc=1, device_id={"tensor": peer_t(k)}, device_id_type=MESH)
-    fac_all[me] = fac_ref[...]
-    cot_all[me] = cot_ref[...]
     pl.semaphore_wait(barrier, n - 1 + T - 1)
 
     def line(buf, ss, rs):
@@ -134,11 +145,17 @@
 
     fac_step, fac_finish, fac_advance = line(fac_all, fac_ss, fac_rs)
     cot_step, cot_finish, cot_advance = line(cot_all, cot_ss, cot_rs)
+    small[0].wait()
+    small[1].wait()
     fac_step(1)
-    cot_step(1)
+    for c in small[2:]:
+        c.wait()
+
+    def row_of(ref):
+        return jnp.concatenate([ref[i:i + 1, :] for i in range(ref.shape[0])], axis=1)
 
     npad = max(16, n)
-    bidx = bidx_ref[...]
+    bidx = row_of(bidx_ref)
     kio = lax.broadcasted_iota(jnp.int32, (npad, slots), 0)
     dest = lax.rem(me + 1 + kio, n)
     first = jnp.where(kio < n, dest * bal, 1 << 24)
@@ -150,7 +167,7 @@
     rank = mm(onehot(hit), tri)
     place = jnp.where(hit, rank, -1.0)
     loc1 = jnp.sum(jnp.where(hit, bidx - first + 1, 0), axis=0, keepdims=True)
-    sidx = sidx_ref[...]
+    sidx = row_of(sidx_ref)
     owner1 = jnp.zeros((1, slots), jnp.int32)
     for a in range(adapters):
         owner1 = jnp.where(sidx == a, slot_ref[a] + 1, owner1)
@@ -186,7 +203,11 @@
                 x_send[g, k - 1] = total.astype(BF16)
                 x_copy(g, k).start()
 
-    steps = [k for k in range(1, n)]
+    hops = [functools.partial(fac_advance, k) for k in range(1, n)]
+    hops[0]()
+    cot_step(1)
+    share = -(-(n - 2) // max(1, G - 1))
+    hops = hops[1:]
     for g in range(G):
         parts = []
         for k in range(g * per, (g + 1) * per):
@@ -212,9 +233,10 @@
             own[g, k] = mm(rows[g], w[H + k])
         if g > 0:
             sum_pair(g - 1)
-        for k in steps[g * (n - 1) // G:(g + 1) * (n - 1) // G]:
-            fac_advance(k)
-            cot_advance(k)
+        for hop in hops[g * share:(g + 1) * share]:
+            hop()
+        if g == G - 2:
+            cot_advance(1)
 
     def select(dense, g):
         total = jnp.zeros((RANK, chunk), F32)
@@ -244,18 +266,6 @@
         low_copy(k, low_send, low_recv, low_ss, low_rs).start()
     sum_pair(G - 1)
 
-    for g in range(G):
-        for i in range(per):
-            k = g * per + i
-            col = loc_cols[k]
-            pick = onehot(
-                col == (lax.broadcasted_iota(jnp.int32, (cap, bal), 1) + 1).astype(F32)
-            )
-            cotb[g, i * cap:(i + 1) * cap, :] = mm(pick, cot_all[peer_dp(k + 1)]).astype(BF16)
-        gl_send[g] = select(mm(up, cotb[g], NT), g)
-    for k in range(1, T):
-        low_copy(k, gl_send, gl_recv, gl_ss, gl_rs).start()
-
     def z_copy(k, send, recv, ss, rs):
         return pltpu.make_async_remote_copy(
             src_ref=send.at[k], dst_ref=recv.at[k],
@@ -266,6 +276,8 @@
     for k in range(n - 1):
         z_copy(k, zm_send, zm_recv, zm_ss, zm_rs).start()
 
+    if n > 2:
+        cot_advance(2)
     for k in range(1, T):
         low_copy(k, low_send, low_recv, low_ss, low_rs).wait_recv()
     up_twice = jnp.concatenate([up, up], axis=0)
@@ -290,6 +302,20 @@
             if k < n - 1:
                 z_copy(k, z_send, z_recv, z_ss, z_rs).start()
 
+    for k in range(3, n):
+        cot_advance(k)
+    for g in range(G):
+        for i in range(per):
+            k = g * per + i
+            col = loc_cols[k]
+            pick = onehot(
+                col == (lax.broadcasted_iota(jnp.int32, (cap, bal), 1) + 1).astype(F32)
+            )
+            cotb[g, i * cap:(i + 1) * cap, :] = mm(pick, cot_all[peer_dp(k + 1)]).astype(BF16)
+        gl_send[g] = select(mm(up, cotb[g], NT), g)
+    for k in range(1, T):
+        low_copy(k, gl_send, gl_recv, gl_ss, gl_rs).start()
+
     for k in range(1, T):
         low_copy(k, gl_send, gl_recv, gl_ss, gl_rs).wait_recv()
     d_down = jnp.zeros((n * RANK, depth), F32)
@@ -326,7 +352,8 @@
     for k in range(1, n):
         g_copy(k).wait_recv()
         total = total + g_recv[k - 1].astype(F32)
-    grad_ref[...] = total
+    down_out[...] = total[:, :depth]
+    up_out[...] = total[:, depth:]
 
     for k in range(1, n):
         fac_finish(k, True)
@@ -351,18 +378,21 @@
     G = 4 if n % 4 == 0 else n
     chunk = n // G * cap
     H = T // 2
-    factors = jnp.concatenate([down.T, up.T], axis=1)
-    vmem, hbm = pl.BlockSpec(memory_space=pltpu.VMEM), pl.BlockSpec(memory_space=pl.ANY)
+    vmem, hbm = pl.BlockSpec(memory_space=pltpu.VMEM), pl.BlockSpec(memory_space=pltpu.HBM)
     dma = pltpu.SemaphoreType.DMA
-    projected, grads = pl.pallas_call(
+    projected, grad_down, grad_up = pl.pallas_call(
         functools.partial(kernel, n, T, G, adapters),
         out_shape=(
             jax.ShapeDtypeStruct((bal, vw), BF16),
-            jax.ShapeDtypeStruct((RANK, depth + vw), F32),
+            jax.ShapeDtypeStruct((RANK, depth), F32),
+            jax.ShapeDtypeStruct((RANK, vw), F32),
         ),
-        in_specs=[pl.BlockSpec(memory_space=pltpu.SMEM), hbm, hbm, vmem, vmem, vmem, vmem],
-        out_specs=(vmem, vmem),
+        in_specs=[hbm] * 8,
+        out_specs=(vmem, vmem, vmem),
         scratch_shapes=[
+            pltpu.SMEM((adapters,), jnp.int32),
+            pltpu.VMEM((slots // 128, 128), jnp.int32),
+            pltpu.VMEM((slots // 128, 128), jnp.int32),
             pltpu.VMEM((slots, depth), BF16),
             pltpu.VMEM((T, depth, vw), BF16),
             pltpu.VMEM((G, chunk, depth), BF16),
@@ -384,6 +414,7 @@
             pltpu.VMEM((n, 8, cap), F32),
             pltpu.VMEM((n, RANK, depth + vw), BF16),
             pltpu.VMEM((n, RANK, depth + vw), BF16),
+            dma((6,)),
             dma((T + 1,)),
             dma((2, n - 1)), dma((2, n - 1)), dma((2, n - 1)), dma((2, n - 1)),
             dma((G,)), dma((G,)), dma((G, H - 1)), dma((G, H - 1)),
@@ -392,14 +423,14 @@
             dma((n - 1,)), dma((n - 1,)),
         ],
         compiler_params=pltpu.CompilerParams(
-            collective_id=0, has_side_effects=True, vmem_limit_bytes=48 * 1024 * 1024
+            collective_id=0, has_side_effects=True, vmem_limit_bytes=60 * 1024 * 1024
         ),
         name="value_lora",
     )(
-        owner_slot, tokens, weight, factors,
-        slot_adapter.reshape(1, slots), balanced.reshape(1, slots), cotangent,
+        owner_slot, tokens, weight, down.T, up.T,
+        slot_adapter.reshape(-1, 128), balanced.reshape(-1, 128), cotangent,
     )
-    return projected, grads[:, :depth].T, grads[:, depth:].T
+    return projected, grad_down.T, grad_up.T
 
 
 def solution(mesh):

time: 52.7 us -> 48.8 us (0.926)
  local copies, waits for them, and re-layouts: 6.8 us -> 4.51 us
  other arithmetic: 0.86 us -> 0 us
  Pallas kernels: 44.1 us -> 43.4 us
    reshape x2 -> x0, local copies, waits for them, and re-layouts: 1.38 us -> none  [the longest x1 0.69 us: body(): slot_adapter.reshape(1, slots)]
    transpose x2 -> x0, local copies, waits for them, and re-layouts: 1.27 us -> none  [body(): return (projected, grads[:, :depth].T, grads[:, depth:].T)]
    concatenate x1 -> x0, other arithmetic: 0.86 us -> none  [body(): factors = jnp.concatenate([down.T, up.T], axis=1)]
    pallas_call x1, Pallas kernels: 44.1 us -> 43.4 us  [body(): pl.pallas_call(functools.partial(kernel, n, T, G, adapters), out_shape=(j...]
    unnamed x7 -> x3, local copies, waits for them, and re-layouts: 4.15 us -> 4.51 us
where the time goes in v2:
time: 48.8 us; the launch traced here: 48.6 us
  Pallas kernels  43.4 us (89%)
  local copies, waits for them, and re-layouts  4.51 us (9%)
  between operations  0.64 us (1%)
    pallas_call x1, Pallas kernels, body(): pl.pallas_call(functools.partial(kernel, n, T, G, adapters), out_shape=(j...  43.4 us
    unnamed x3, local copies, waits for them, and re-layouts  4.51 us

profile of v2, /device:TPU:1, one launch (start us, length us, event | category | flops | bytes accessed | tf_op | source)
XLA Modules:
  0.0 48.6 jit_solution(16119850405269421894)
XLA Ops:
  0.6 43.4 %value_lora.1 = (bf16[384,256]{1,0:T(8,128)(2,1)}, f32[16,2048]{1,0:T(8,128)}, f32[16,256]{1,0:T(8,128)}) custom-call(s32[4]{0:T(128)} %slot_hbm.1, bf16[768,2048]{1,0:T(8,128)(2,1)} %tok_hbm.1, bf16[2048,1024]{1,0:T(8,128)(2,1)} %w_hbm.1, bf16[16,2048]{1,0:T(8,128)(2,1)} %bitcast.7, bf16[16,256]{1,0:T(8,128)(2,1)} %bitcast.9, s32[6,128]{1,0:T(8,128)} %bitcast.10, ...), custom_call_target="tpu_custom_call" | custom-call | tf_op jit(solution)/shard_map/value_lora/pallas_call | solution.py:383
  44.1 1.6 %copy.14 = bf16[384,256]{1,0:T(8,128)(2,1)} copy(bf16[384,256]{1,0:T(8,128)(2,1)} %get-tuple-element.12) | data formatting | bytes 393216
  45.7 1.6 %copy.15 = f32[2048,16]{0,1:T(8,128)} copy(f32[2048,16]{0,1:T(8,128)} %bitcast.6) | data formatting | bytes 262144
  47.3 1.3 %copy.16 = f32[256,16]{0,1:T(8,128)} copy(f32[256,16]{0,1:T(8,128)} %bitcast.8) | data formatting | bytes 32768
